TPU v7x, 512 devices: a whole 4x8x8 slice. The times are simulated.
512 devices in a mesh: dom: 32 (over x, z), bal: 16 (over y, core).
Axes of the slice: x: 4, y: 8, z: 8, core: 2. Of those that a mesh axis runs over, the one named last changes fastest.
Arguments:
- edge_wind: bfloat16 [55, 1572864], P(None, ('dom', 'bal')), may hold values from -6 to 6
- send_edges: int32 [2, 131072], P(None, ('dom', 'bal')), may hold values from 0 to 3071, as said below
- stencil: int32 [10, 524288], P(None, ('dom', 'bal')), may hold values from 0 to 3581, as said below
- rbf_coeff: float32 [2, 10, 524288], P(None, None, ('dom', 'bal')), may hold values from -2 to 2
- state: float32 [4, 55, 524288], P(None, None, ('dom', 'bal')), may hold values from 0 to 2
- rain_cols: int32 [262144], P(('dom', 'bal')), may hold values from 0 to 1023, as said below
- rain_count: int32 [512], P(('dom', 'bal')), may hold values from 0 to 512, as said below
Outputs:
- cell_wind: bfloat16 [2, 55, 524288], P(None, None, ('dom', 'bal'))
- tendency: float32 [4, 55, 524288], P(None, None, ('dom', 'bal'))
Inputs may be any that keep to these rules, and one draw needn't show every extreme that they name: `send_edges`: entries are own edge numbers of the sending partition. `stencil`: numbers index the extended edge list of the cell's partition: 256 received from the preceding partition along dom, its own 3072, then 256 from the following one. The entries of local cell n lie between 3 n and 3 n + 512. `rain_cols`: each partition's block holds distinct local cell numbers; entries at and beyond its count are unused. `rain_count`: two partitions whose bal indices differ only in the lowest bit hold exactly 512 precipitating cells together.
All inputs are finite; a program needn't handle non-finite values.
Results may differ from a plain program's by a relative error of at most 0.0065.
Values may be sent and summed in bfloat16 or wider, within the bound.
No kernel may reach another device: no remote copies, remote signals or barrier semaphores. Data moves between devices by JAX's collectives and lax.ppermute only.
A program may use at most 64 MiB of HBM per device.

v0:
```python
import math

import jax
import jax.numpy as jnp
from jax import lax
from jax.sharding import PartitionSpec as P

NSUB = 3


def padded(cells, sides, width):
    for axis, dim in sides:
        count = lax.axis_size(axis)
        head = lax.slice_in_dim(cells, 0, width, axis=dim)
        tail = lax.slice_in_dim(cells, cells.shape[dim] - width, cells.shape[dim], axis=dim)
        cells = jnp.concatenate(
            [
                lax.ppermute(tail, axis, [(i, (i + 1) % count) for i in range(count)]),
                cells,
                lax.ppermute(head, axis, [((i + 1) % count, i) for i in range(count)]),
            ],
            axis=dim,
        )
    return cells


def partner(block, axis, stride):
    count = lax.axis_size(axis)
    route = []
    for low in range(count):
        high = low | 1 << stride
        if high != low and high < count:
            route += [(low, high), (high, low)]
    return lax.ppermute(block, axis, route)


def shortened(shard):
    return jax.tree.map(lambda a: a.astype(jnp.bfloat16) if a.dtype == jnp.float32 else a, shard)


def saturate(temper, vapour, cloud_water, rain_water):
    saturation = jnp.exp(0.3 * temper)
    condensed = jnp.maximum((vapour - saturation) / (1.0 + 0.45 * saturation), -cloud_water)
    return (temper + 0.8 * condensed, vapour - condensed, cloud_water + condensed, rain_water)


def rainfall(temper, vapour, cloud_water, rain_water, airspeed):
    levels = temper.shape[0]
    height = jnp.exp(jnp.arange(levels, dtype=jnp.float32) / levels)[:, None]
    falloff = math.exp(-1.0 / levels)
    for substep in range(NSUB):
        saturation = jnp.exp(0.3 * temper)
        collected = 0.5 * jnp.maximum(cloud_water - 0.5, 0.0) + 1.5 * cloud_water * jnp.power(
            rain_water, 0.875
        )
        sink_rate = jnp.minimum(collected, cloud_water)
        evaporate = (
            0.3
            * (1.0 + 0.25 * airspeed)
            * jnp.maximum(saturation - vapour, 0.0)
            * jnp.power(rain_water, 0.525)
        )
        evaporate = jnp.minimum(evaporate, rain_water)
        temper = temper - 0.8 * evaporate
        vapour = vapour + evaporate
        cloud_water = cloud_water - sink_rate
        middle = rain_water + sink_rate - evaporate
        falling = jnp.minimum(0.5 * jnp.power(middle, 0.1364) * height, 0.9) * middle
        inflow = jnp.concatenate([falling[1:] * falloff, jnp.zeros_like(falling[:1])], axis=0)
        rain_water = middle - falling + inflow
    return (temper, vapour, cloud_water, rain_water)


def reconstruct(extended, stencil, rbf_coeff, halo_width):
    levels = extended.shape[0]
    cell_count = stencil.shape[1]
    block_cells = 128
    block_total = cell_count // block_cells
    window = 3 * block_cells + 2 * halo_width
    positions = jnp.arange(window, dtype=jnp.int32)

    def one_block(block_id):
        first_cell = block_id * block_cells
        first_edge = 3 * first_cell
        edge_window = lax.dynamic_slice_in_dim(extended, first_edge, window, 1).astype(jnp.float32)
        members = lax.dynamic_slice_in_dim(stencil, first_cell, block_cells, 1) - first_edge
        weights = lax.dynamic_slice_in_dim(rbf_coeff, first_cell, block_cells, 2)
        selector = (positions[None, :, None] == members[:, None, :]).astype(jnp.float32)
        zonal_table = jnp.sum(weights[0][:, None, :] * selector, axis=0)
        meridional_table = jnp.sum(weights[1][:, None, :] * selector, axis=0)
        tables = jnp.concatenate([zonal_table, meridional_table], axis=1)
        return jnp.dot(
            edge_window, tables, precision=lax.Precision.HIGHEST, preferred_element_type=jnp.float32
        )

    blocks = lax.map(one_block, jnp.arange(block_total, dtype=jnp.int32))
    blocks = blocks.reshape(block_total, levels, 2, block_cells)
    return jnp.transpose(blocks, (2, 1, 0, 3)).reshape(2, levels, cell_count)


def local(edge_wind, send_edges, stencil, rbf_coeff, state, rain_cols, rain_count):
    halo_width = send_edges.shape[1]
    levels = edge_wind.shape[0]
    outgoing = jnp.concatenate(
        [jnp.take(edge_wind, send_edges[0], axis=1), jnp.take(edge_wind, send_edges[1], axis=1)],
        axis=1,
    )
    bordered = padded(outgoing, (("dom", 1),), halo_width)
    extended = jnp.concatenate(
        [bordered[:, :halo_width], edge_wind, bordered[:, 3 * halo_width :]], axis=1
    )
    cell_count = stencil.shape[1]
    cell_wind = reconstruct(extended, stencil, rbf_coeff, halo_width).astype(jnp.bfloat16)
    wind_float = cell_wind.astype(jnp.float32)
    airspeed = jnp.sqrt(wind_float[0] * wind_float[0] + wind_float[1] * wind_float[1] + 1.0)
    adjusted = saturate(state[0], state[1], state[2], state[3])
    live_count = rain_count[0]
    list_length = rain_cols.shape[0]
    slot_ids = jnp.arange(list_length, dtype=jnp.int32)
    picker = (jnp.arange(cell_count, dtype=jnp.int32)[:, None] == rain_cols[None, :]).astype(
        jnp.float32
    )
    fields_all = jnp.concatenate(adjusted + (airspeed,), axis=0)
    picked_all = jnp.dot(
        fields_all, picker, precision=lax.Precision.HIGHEST, preferred_element_type=jnp.float32
    )
    picked_all = picked_all.reshape(5, levels, list_length)
    halfway = list_length // 2
    arrived = partner(picked_all[:, :, halfway:].astype(jnp.bfloat16), "bal", 0).astype(jnp.float32)
    first_slots = slot_ids[:halfway]
    source = jnp.clip(first_slots - live_count, 0, halfway - 1)
    borrowed = jnp.take(arrived, source, axis=2)
    working = jnp.where(
        (first_slots < live_count)[None, None, :], picked_all[:, :, :halfway], borrowed
    )
    computed = jnp.stack(rainfall(working[0], working[1], working[2], working[3], working[4]))
    back_index = jnp.clip(live_count + first_slots, 0, halfway - 1)
    returned = partner(shortened(jnp.take(computed, back_index, axis=2)), "bal", 0)
    merged = jnp.concatenate([computed, returned], axis=2)
    results = (merged[0], merged[1], merged[2], merged[3])
    live_mask = (slot_ids < live_count).astype(jnp.float32)
    live_results = jnp.concatenate(results, axis=0) * live_mask[None, :]
    placed = jnp.dot(
        live_results, picker.T, precision=lax.Precision.HIGHEST, preferred_element_type=jnp.float32
    )
    covered = (
        jnp.dot(
            picker, live_mask, precision=lax.Precision.HIGHEST, preferred_element_type=jnp.float32
        )
        > 0.5
    )
    adjusted_all = jnp.stack(adjusted).reshape(4 * levels, cell_count)
    updated = jnp.where(covered[None, :], placed, adjusted_all).reshape(4, levels, cell_count)
    return (cell_wind, updated - state)


def solution(mesh):
    placed = (
        P(None, ("dom", "bal")),
        P(None, ("dom", "bal")),
        P(None, ("dom", "bal")),
        P(None, None, ("dom", "bal")),
        P(None, None, ("dom", "bal")),
        P(("dom", "bal")),
        P(("dom", "bal")),
    )
    return jax.shard_map(
        local,
        mesh=mesh,
        in_specs=placed,
        out_specs=(P(None, None, ("dom", "bal")), P(None, None, ("dom", "bal"))),
        check_vma=False,
    )
```

profile of v0, /device:TPU:1, one launch (start us, length us, event | category | flops | bytes accessed | tf_op | source)
XLA Modules:
  0.0 112.7 jit_solution(3599749352106771759)
XLA Ops:
  1.4 1.4 %copy.90 = bf16[55,3072]{0,1:T(8,128)(2,1)S(1)} copy(bf16[55,3072]{1,0:T(8,128)(2,1)} %param.11) | data formatting | bytes 675840 | tf_op args[0]
  3.8 4.8 %collective-permute-start = (bf16[55,256]{0,1:T(8,128)(2,1)S(1)}, bf16[55,256]{0,1:T(8,128)(2,1)S(1)}, u32[]{:S(2)}, u32[]{:S(2)}) collective-permute-start(bf16[55,256]{0,1:T(8,128)(2,1)S(1)} %select_bitcast_fusion.1), channel_id=1, source_target_pairs={{0,16},{16,32},{32,48},{48,64},{64,80},{80,96},{96,112},{112,128},... | collective-permute-start | bytes 84488 | tf_op jit(solution)/shard_map/ppermute | solution.py:18
  9.6 10.8 %collective-permute-start.1 = (bf16[55,256]{0,1:T(8,128)(2,1)S(1)}, bf16[55,256]{0,1:T(8,128)(2,1)S(1)}, u32[]{:S(2)}, u32[]{:S(2)}) collective-permute-start(bf16[55,256]{0,1:T(8,128)(2,1)S(1)} %select_bitcast_fusion), channel_id=1, source_target_pairs={{16,0},{32,16},{48,32},{64,48},{80,64},{96,80},{112,96},{128,112},... | collective-permute-start | bytes 84488 | tf_op jit(solution)/shard_map/ppermute | solution.py:20
  26.1 58.0 %while.13 = (s32[]{:T(128)}, bf16[8,55,256]{2,0,1:T(8,128)(2,1)}, s32[8]{0:T(128)S(1)}, bf16[55,3584]{1,0:T(8,128)(2,1)S(1)}, s32[10,1024]{1,0:T(8,128)}, /*inde...) while((s32[]{:T(128)}, bf16[8,55,256]{2,0,1:T(8,128)(2,1)}, ...), condition=%wide.region_3.5_spmd.clone, body=%wide.region_0.4_spmd.clone.sunk | while | flops 157123856 | bytes 2142985 | solution.py:96
  31.0 2.3 %dynamic_update_slice.9 = bf16[8,55,256]{2,0,1:T(8,128)(2,1)} dynamic-update-slice(bf16[8,55,256]{2,0,1:T(8,128)(2,1)} %get-tuple-element.259, bf16[1,55,256]{2,0,1:T(2,128)(2,1)S(1)} %copy.122, s32[]{:T(128)} %get-tuple-element.258, s32[]{:T(128)} %constant.109.clone.1..sunk, s32[]{:T(128)} %constant.109.clone.1..sunk) | dynamic-update-slice | bytes 56324 | tf_op jit(solution)/shard_map/while/body/jit(dynamic_update_index_in_dim)/dynamic_update_slice | solution.py:96
  38.3 2.3 %dynamic_update_slice.9 = bf16[8,55,256]{2,0,1:T(8,128)(2,1)} dynamic-update-slice(bf16[8,55,256]{2,0,1:T(8,128)(2,1)} %get-tuple-element.259, bf16[1,55,256]{2,0,1:T(2,128)(2,1)S(1)} %copy.122, s32[]{:T(128)} %get-tuple-element.258, s32[]{:T(128)} %constant.109.clone.1..sunk, s32[]{:T(128)} %constant.109.clone.1..sunk) | dynamic-update-slice | bytes 56324 | tf_op jit(solution)/shard_map/while/body/jit(dynamic_update_index_in_dim)/dynamic_update_slice | solution.py:96
  45.5 2.3 %dynamic_update_slice.9 = bf16[8,55,256]{2,0,1:T(8,128)(2,1)} dynamic-update-slice(bf16[8,55,256]{2,0,1:T(8,128)(2,1)} %get-tuple-element.259, bf16[1,55,256]{2,0,1:T(2,128)(2,1)S(1)} %copy.122, s32[]{:T(128)} %get-tuple-element.258, s32[]{:T(128)} %constant.109.clone.1..sunk, s32[]{:T(128)} %constant.109.clone.1..sunk) | dynamic-update-slice | bytes 56324 | tf_op jit(solution)/shard_map/while/body/jit(dynamic_update_index_in_dim)/dynamic_update_slice | solution.py:96
  52.8 2.3 %dynamic_update_slice.9 = bf16[8,55,256]{2,0,1:T(8,128)(2,1)} dynamic-update-slice(bf16[8,55,256]{2,0,1:T(8,128)(2,1)} %get-tuple-element.259, bf16[1,55,256]{2,0,1:T(2,128)(2,1)S(1)} %copy.122, s32[]{:T(128)} %get-tuple-element.258, s32[]{:T(128)} %constant.109.clone.1..sunk, s32[]{:T(128)} %constant.109.clone.1..sunk) | dynamic-update-slice | bytes 56324 | tf_op jit(solution)/shard_map/while/body/jit(dynamic_update_index_in_dim)/dynamic_update_slice | solution.py:96
  60.0 2.3 %dynamic_update_slice.9 = bf16[8,55,256]{2,0,1:T(8,128)(2,1)} dynamic-update-slice(bf16[8,55,256]{2,0,1:T(8,128)(2,1)} %get-tuple-element.259, bf16[1,55,256]{2,0,1:T(2,128)(2,1)S(1)} %copy.122, s32[]{:T(128)} %get-tuple-element.258, s32[]{:T(128)} %constant.109.clone.1..sunk, s32[]{:T(128)} %constant.109.clone.1..sunk) | dynamic-update-slice | bytes 56324 | tf_op jit(solution)/shard_map/while/body/jit(dynamic_update_index_in_dim)/dynamic_update_slice | solution.py:96
  67.3 2.3 %dynamic_update_slice.9 = bf16[8,55,256]{2,0,1:T(8,128)(2,1)} dynamic-update-slice(bf16[8,55,256]{2,0,1:T(8,128)(2,1)} %get-tuple-element.259, bf16[1,55,256]{2,0,1:T(2,128)(2,1)S(1)} %copy.122, s32[]{:T(128)} %get-tuple-element.258, s32[]{:T(128)} %constant.109.clone.1..sunk, s32[]{:T(128)} %constant.109.clone.1..sunk) | dynamic-update-slice | bytes 56324 | tf_op jit(solution)/shard_map/while/body/jit(dynamic_update_index_in_dim)/dynamic_update_slice | solution.py:96
  74.5 2.3 %dynamic_update_slice.9 = bf16[8,55,256]{2,0,1:T(8,128)(2,1)} dynamic-update-slice(bf16[8,55,256]{2,0,1:T(8,128)(2,1)} %get-tuple-element.259, bf16[1,55,256]{2,0,1:T(2,128)(2,1)S(1)} %copy.122, s32[]{:T(128)} %get-tuple-element.258, s32[]{:T(128)} %constant.109.clone.1..sunk, s32[]{:T(128)} %constant.109.clone.1..sunk) | dynamic-update-slice | bytes 56324 | tf_op jit(solution)/shard_map/while/body/jit(dynamic_update_index_in_dim)/dynamic_update_slice | solution.py:96
  81.7 2.3 %dynamic_update_slice.9 = bf16[8,55,256]{2,0,1:T(8,128)(2,1)} dynamic-update-slice(bf16[8,55,256]{2,0,1:T(8,128)(2,1)} %get-tuple-element.259, bf16[1,55,256]{2,0,1:T(2,128)(2,1)S(1)} %copy.122, s32[]{:T(128)} %get-tuple-element.258, s32[]{:T(128)} %constant.109.clone.1..sunk, s32[]{:T(128)} %constant.109.clone.1..sunk) | dynamic-update-slice | bytes 56324 | tf_op jit(solution)/shard_map/while/body/jit(dynamic_update_index_in_dim)/dynamic_update_slice | solution.py:96
  84.0 1.0 convert_element_type.38
  85.9 3.4 %concatenate.28 = f32[275,1024]{1,0:T(8,128)S(1)} concatenate(f32[55,1024]{1,0:T(8,128)} %get-tuple-element.176, f32[55,1024]{1,0:T(8,128)} %get-tuple-element.175, f32[55,1024]{1,0:T(8,128)S(1)} %copy-done.2, f32[55,1024]{1,0:T(8,128)S(1)} %get-tuple-element.179, f32[55,1024]{1,0:T(8,128)} %fusion.28), dimensions={0} | concatenate | bytes 2252800 | tf_op jit(solution)/shard_map/concatenate | solution.py:123
  89.4 2.1 %fusion.13 = f32[275,512]{1,0:T(8,128)} fusion(f32[275,1024]{1,0:T(8,128)S(1)} %concatenate.28, s32[512]{0:T(512)S(1)} %copy-done.8), kind=kOutput, calls=%fused_computation.24 | convolution fusion | flops 1730674688 | bytes 1691648 | tf_op jit(solution)/shard_map/dot_general | solution.py:124
  91.4 1.1 reshape.65
  92.6 2.9 %collective-permute-start.2 = (bf16[5,55,256]{2,1,0:T(8,128)(2,1)S(1)}, bf16[5,55,256]{2,1,0:T(8,128)(2,1)}, u32[]{:S(2)}, u32[]{:S(2)}) collective-permute-start(bf16[5,55,256]{2,1,0:T(8,128)(2,1)S(1)} %slice.233), channel_id=1, source_target_pairs={{0,1},{1,0},{2,3},{3,2},{4,5},{5,4},{6,7},{7,6},{8,9},{9,8},{10,11... | collective-permute-start | bytes 422408 | tf_op jit(solution)/shard_map/ppermute | solution.py:34
  96.6 1.3 %copy.101 = f32[5,55,256]{1,0,2:T(8,128)S(1)} copy(bf16[5,55,256]{2,1,0:T(8,128)(2,1)} %collective-permute-done.2) | data formatting | bytes 422400 | tf_op jit(solution)/shard_map/convert_element_type | solution.py:129
  97.9 2.0 %gather_fusion = f32[256,5,55]{2,1,0:T(8,128)} fusion(f32[5,55,256]{1,0,2:T(8,128)S(1)} %copy.101, s32[1024]{0:T(1024)S(1)} %pad_clamp_fusion.1), kind=kCustom, calls=%fused_computation.2 | custom fusion | bytes 564224 | tf_op jit(solution)/shard_map/jit(_take)/gather | solution.py:132
  99.9 1.5 %copy.102 = f32[256,5,55]{0,2,1:T(8,128)S(1)} copy(f32[256,5,55]{2,1,0:T(8,128)} %gather_fusion) | data formatting | bytes 563200 | tf_op jit(solution)/shard_map/jit(_take)/gather | solution.py:132
  103.8 2.3 %collective-permute-start.3 = (bf16[4,55,256]{2,1,0:T(8,128)(2,1)S(1)}, bf16[4,55,256]{2,1,0:T(8,128)(2,1)S(1)}, u32[]{:S(2)}, u32[]{:S(2)}) collective-permute-start(bf16[4,55,256]{2,1,0:T(8,128)(2,1)S(1)} %fusion.33), channel_id=1, source_target_pairs={{0,1},{1,0},{2,3},{3,2},{4,5},{5,4},{6,7},{7,6},{8,9},{9,8},{10,11... | collective-permute-start | bytes 337928 | tf_op jit(solution)/shard_map/ppermute | solution.py:34
  107.2 2.2 %fusion.15 = f32[220,1024]{1,0:T(8,128)} fusion(f32[220,1024]{1,0:T(8,128)S(1)} %reshape.66, s32[512]{0:T(512)S(1)} %copy-done.9, f32[55,512]{1,0:T(8,128)S(1)} %get-tuple-element.184, f32[55,512]{1,0:T(8,128)S(1)} %get-tuple-element.185, f32[55,512]{1,0:T(8,128)S(1)} %get-tuple-element.186, f32[55,512]{1,0:T(8,128)S(1)} %get-tuple-element.183, ...), kind=kOutput, calls=%fused_computation.26 | convolution fusion | flops 1385320448 | bytes 2257920 | tf_op jit(solution)/shard_map/dot_general | solution.py:143
  109.4 1.3 %reshape.67 = f32[4,55,1024]{2,1,0:T(8,128)S(1)} reshape(f32[220,1024]{1,0:T(8,128)} %fusion.15) | data formatting | bytes 1802240 | tf_op jit(solution)/shard_map/reshape | solution.py:153
  111.2 1.5 %copy.106 = f32[4,55,1024]{2,0,1:T(4,128)} copy(f32[4,55,1024]{2,1,0:T(8,128)S(1)} %copy_subtract_fusion) | data formatting | bytes 1802240
  (133 shorter events, 42.9 us)
Async XLA Ops:
  0.6 19.8 %copy-start = (f32[4,55,1024]{2,0,1:T(4,128)S(1)}, f32[4,55,1024]{2,0,1:T(4,128)}, u32[]{:S(2)}) copy-start(f32[4,55,1024]{2,0,1:T(4,128)} %param.15) | copy-start | bytes 2703364
  3.8 21.4 %collective-permute-start = (bf16[55,256]{0,1:T(8,128)(2,1)S(1)}, bf16[55,256]{0,1:T(8,128)(2,1)S(1)}, u32[]{:S(2)}, u32[]{:S(2)}) collective-permute-start(bf16[55,256]{0,1:T(8,128)(2,1)S(1)} %select_bitcast_fusion.1), channel_id=1, source_target_pairs={{0,16},{16,32},{32,48},{48,64},{64,80},{80,96},{96,112},{112,128},... | collective-permute-start | bytes 84488 | tf_op jit(solution)/shard_map/ppermute | solution.py:18
  9.6 15.6 %collective-permute-start.1 = (bf16[55,256]{0,1:T(8,128)(2,1)S(1)}, bf16[55,256]{0,1:T(8,128)(2,1)S(1)}, u32[]{:S(2)}, u32[]{:S(2)}) collective-permute-start(bf16[55,256]{0,1:T(8,128)(2,1)S(1)} %select_bitcast_fusion), channel_id=1, source_target_pairs={{16,0},{32,16},{48,32},{64,48},{80,64},{96,80},{112,96},{128,112},... | collective-permute-start | bytes 84488 | tf_op jit(solution)/shard_map/ppermute | solution.py:20
  21.9 2.7 %copy-start.8 = (s32[512]{0:T(512)S(1)}, s32[512]{0:T(512)}, u32[]{:S(2)}) copy-start(s32[512]{0:T(512)} %param.16) | copy-start | bytes 6148
  25.1 1.0 copy-start.1
  84.0 1.9 %copy-start.2 = (f32[55,1024]{1,0:T(8,128)S(1)}, f32[55,1024]{1,0:T(8,128)}, u32[]{:S(2)}) copy-start(f32[55,1024]{1,0:T(8,128)} %get-tuple-element.167) | copy-start | bytes 675844
  85.1 0.8 copy-start.3
  92.6 4.0 %collective-permute-start.2 = (bf16[5,55,256]{2,1,0:T(8,128)(2,1)S(1)}, bf16[5,55,256]{2,1,0:T(8,128)(2,1)}, u32[]{:S(2)}, u32[]{:S(2)}) collective-permute-start(bf16[5,55,256]{2,1,0:T(8,128)(2,1)S(1)} %slice.233), channel_id=1, source_target_pairs={{0,1},{1,0},{2,3},{3,2},{4,5},{5,4},{6,7},{7,6},{8,9},{9,8},{10,11... | collective-permute-start | bytes 422408 | tf_op jit(solution)/shard_map/ppermute | solution.py:34
  97.8 3.5 %copy-start.6 = (pred[256]{0:T(512)(128)(4,1)S(1)}, pred[256]{0:T(512)(128)(4,1)}, u32[]{:S(2)}) copy-start(pred[256]{0:T(512)(128)(4,1)} %get-tuple-element.189) | copy-start | bytes 772
  97.8 3.5 %copy-start.7 = (pred[256]{0:T(512)(128)(4,1)S(1)}, pred[256]{0:T(512)(128)(4,1)}, u32[]{:S(2)}) copy-start(pred[256]{0:T(512)(128)(4,1)} %get-tuple-element.191) | copy-start | bytes 772
  102.0 1.8 %copy-start.4 = (pred[256]{0:T(512)(128)(4,1)S(1)}, pred[256]{0:T(512)(128)(4,1)}, u32[]{:S(2)}) copy-start(pred[256]{0:T(512)(128)(4,1)} %get-tuple-element.153) | copy-start | bytes 772
  103.8 3.4 %copy-start.5 = (f32[512]{0:T(512)S(1)}, f32[512]{0:T(512)}, u32[]{:S(2)}) copy-start(f32[512]{0:T(512)} %get-tuple-element.195) | copy-start | bytes 6148
  103.8 3.4 %copy-start.9 = (s32[512]{0:T(512)S(1)}, s32[512]{0:T(512)}, u32[]{:S(2)}) copy-start(s32[512]{0:T(512)} %param.16) | copy-start | bytes 6148
  103.8 3.2 %collective-permute-start.3 = (bf16[4,55,256]{2,1,0:T(8,128)(2,1)S(1)}, bf16[4,55,256]{2,1,0:T(8,128)(2,1)S(1)}, u32[]{:S(2)}, u32[]{:S(2)}) collective-permute-start(bf16[4,55,256]{2,1,0:T(8,128)(2,1)S(1)} %fusion.33), channel_id=1, source_target_pairs={{0,1},{1,0},{2,3},{3,2},{4,5},{5,4},{6,7},{7,6},{8,9},{9,8},{10,11... | collective-permute-start | bytes 337928 | tf_op jit(solution)/shard_map/ppermute | solution.py:34
where the time goes:
time: 114 us; the launch traced here: 113 us
  local copies, waits for them, and re-layouts  50.7 us (44%)
  starting transfers between devices  20.8 us (18%)
  other arithmetic  19.1 us (17%)
  loops' own time  10.3 us (9%)
  matrix products  8.24 us (7%)
  waiting for transfers between devices  1.9 us (2%)
  between operations  1.7 us (1%)
    dynamic_update_slice x16, local copies, waits for them, and re-layouts, reconstruct(): blocks = lax.map(one_block, jnp.arange(block_total, dtype=jnp.int32))  18.7 us
    ppermute x1, starting transfers between devices, padded(): lax.ppermute(head, axis, [((i + 1) % count, i) for i in range(count)])  10.8 us
    another operation x1, loops' own time, reconstruct(): blocks = lax.map(one_block, jnp.arange(block_total, dtype=jnp.int32))  10.3 us
    reduce_sum x8, other arithmetic, one_block(): zonal_table = jnp.sum(weights[0][:, None, :] * selector, axis=0)  7.73 us
    slice x8, local copies, waits for them, and re-layouts, one_block(): meridional_table = jnp.sum(weights[1][:, None, :] * selector, axis=0)  6.9 us
    sub x8, other arithmetic, one_block(): lax.dynamic_slice_in_dim(stencil, first_cell, block_cells, 1) - first_edge  5.68 us
    ppermute x2, starting transfers between devices, partner(): return lax.ppermute(block, axis, route)  5.15 us
    dynamic_slice x8, local copies, waits for them, and re-layouts, reconstruct(): blocks = lax.map(one_block, jnp.arange(block_total, dtype=jnp.int32))  5.09 us
  transfers between devices with their start and end apart: 4, of which 2 were waited for; matrix products, arithmetic and copies ran while one was open for 5% of the time, Pallas kernels for 0%

commit v1 on v0

v1 whole, which is shorter than its diff:
```python
import math

import jax
import jax.numpy as jnp
from jax import lax
from jax.experimental import pallas as pl
from jax.experimental.pallas import tpu as pltpu
from jax.sharding import PartitionSpec as P

NSUB = 3
LOG2E = math.log2(math.e)
LANES = 128
ROWS = 16
PIECES = 4
VMEM_BYTES = 40 * 1024 * 1024
RING = 8


def pick_sends(send_ref, edge_ref, arrivals, left_ref, right_ref, stack_ref, found_ref):
    edges = edge_ref.shape[1]
    width = send_ref.shape[1]
    chunk = 256
    span = edges // len(arrivals)
    wanted = jnp.concatenate([send_ref[0:1, :], send_ref[1:2, :]], axis=1)
    low = jnp.broadcast_to(lax.rem(wanted, chunk), (ROWS, 2 * width)).astype(jnp.int16)
    high = jnp.broadcast_to(wanted // chunk, (8, 2 * width))
    rows = lax.broadcasted_iota(jnp.int32, (ROWS, 2 * width), 0)
    picker = jnp.concatenate(
        [
            jnp.where(low == (rows + row).astype(jnp.int16), jnp.bfloat16(1), jnp.bfloat16(0))
            for row in range(0, chunk, ROWS)
        ],
        axis=0,
    )
    levels = edge_ref.shape[0]
    step = stack_ref.shape[0] // (edges // chunk)
    for first in range(0, edges, chunk):
        if first % span == 0:
            arrivals[first // span].wait()
        base = first // chunk * step
        stack_ref[base : base + levels, :] = edge_ref[:, first : first + chunk]
    for side, out_ref in ((0, left_ref), (1, right_ref)):
        columns = slice(side * width, (side + 1) * width)
        found_ref[...] = jnp.dot(
            stack_ref[...], picker[:, columns], preferred_element_type=jnp.float32
        )
        here = [high[:, columns] == n for n in range(edges // chunk)]
        total = []
        for base in range(0, levels, 8):
            some = found_ref[base : base + 8, :]
            for n in range(1, edges // chunk):
                some = jnp.where(here[n], found_ref[n * step + base : n * step + base + 8, :], some)
            total.append(some)
        out_ref[...] = jnp.concatenate(total, axis=0)[:levels].astype(jnp.bfloat16)


def listed_mask(cols_ref, count):
    slots = cols_ref.shape[1]
    cols = cols_ref[...]
    live = lax.broadcasted_iota(jnp.int32, (1, slots), 1) < count
    high = jnp.where(live, cols // LANES, -1)
    low = lax.rem(cols, LANES)
    rows = jnp.where(lax.broadcasted_iota(jnp.int32, (8, slots), 0) == high, 1.0, 0.0)
    lanes = jnp.where(lax.broadcasted_iota(jnp.int32, (LANES, slots), 0) == low, 1.0, 0.0)
    return lax.dot_general(
        rows.astype(jnp.bfloat16),
        lanes.astype(jnp.bfloat16),
        (((1,), (1,)), ((), ())),
        preferred_element_type=jnp.float32,
    )


def merge_members(sten_ref, rbf_ref, pos_ref, zon_ref, mer_ref, tmp_ref, fold):
    members = sten_ref.shape[0]
    blocks = sten_ref.shape[1] // LANES
    for k in range(blocks):
        tmp_ref[ROWS * k : ROWS * k + members, :] = (
            sten_ref[:, LANES * k : LANES * (k + 1)] - 3 * LANES * k
        )
    places, zonal, merid = [], [], []
    for s in range(members):
        places.append(tmp_ref[pl.ds(s, blocks, stride=ROWS), :])
        zonal.append(rbf_ref[pl.ds(2 * blocks * s, blocks, stride=2), :])
        merid.append(rbf_ref[pl.ds(2 * blocks * s + 1, blocks, stride=2), :])
    for t in range(members):
        z, m = zonal[t], merid[t]
        for s in range(t):
            same = places[s] == places[t]
            z = z + jnp.where(same, zonal[s], 0.0)
            m = m + jnp.where(same, merid[s], 0.0)
        rows = slice(blocks * t, blocks * (t + 1))
        pos_ref[rows, :] = jnp.where(places[t] >= fold, places[t] - fold, places[t])
        zon_ref[rows, :] = z
        mer_ref[rows, :] = m


def build_table(k, members, blocks, fold, window, pos_ref, zon_ref, mer_ref, table_ref):
    def spread(ref, s, kind):
        row = ref[pl.ds(blocks * s + k, 1), :]
        return jnp.broadcast_to(row, (ROWS, LANES)).astype(kind)

    places = [spread(pos_ref, s, jnp.int16) for s in range(members)]
    zonal = [spread(zon_ref, s, jnp.bfloat16) for s in range(members)]
    merid = [spread(mer_ref, s, jnp.bfloat16) for s in range(members)]
    rows = lax.broadcasted_iota(jnp.int32, (ROWS, LANES), 0)
    first = (3 * lax.broadcasted_iota(jnp.int32, (ROWS, LANES), 1)).astype(jnp.int16)
    none = jnp.zeros((ROWS, LANES), jnp.bfloat16)
    for row in range(0, fold, ROWS):
        here = (rows + row).astype(jnp.int16)
        z, m = none, none
        for s in range(members):
            hit = places[s] == here
            z = jnp.where(hit, zonal[s], z)
            m = jnp.where(hit, merid[s], m)
        if row + fold < window:
            low = first <= here
            table_ref[row : row + ROWS, :LANES] = jnp.where(low, z, none)
            table_ref[row : row + ROWS, LANES:] = jnp.where(low, m, none)
            table_ref[fold + row : fold + row + ROWS, :LANES] = jnp.where(low, none, z)
            table_ref[fold + row : fold + row + ROWS, LANES:] = jnp.where(low, none, m)
        else:
            table_ref[row : row + ROWS, :LANES] = z
            table_ref[row : row + ROWS, LANES:] = m


def keep_wind(k, levels, blocks, wind, wide_ref):
    for base in range(0, levels, 8):
        count = min(8, levels - base)
        for c in range(2):
            wide_ref[pl.ds(2 * (blocks * base + k) + c, count, stride=2 * blocks), :] = wind[
                base : base + count, LANES * c : LANES * (c + 1)
            ]


def rain_column(k, levels, blocks, listed, wind, state_ref, tend_ref, dry_ref):
    if listed is not None:
        listed = jnp.broadcast_to(listed, (8, LANES)) > 0.5
    falloff = math.exp(-1.0 / levels)
    stride = 4 * blocks
    above = [None] * NSUB
    for base in reversed(range(0, levels, 8)):
        count = min(8, levels - base)
        u = wind[base : base + count, :LANES]
        v = wind[base : base + count, LANES:]
        airspeed = jnp.sqrt(u * u + v * v + 1.0)
        factor = 0.3 + 0.075 * airspeed
        before = [
            state_ref[pl.ds(stride * base + 4 * k + f, count, stride=stride), :] for f in range(4)
        ]
        t, qv, qc, qr = before
        qvs = jnp.exp2((0.3 * LOG2E) * t)
        cond = jnp.maximum((qv - qvs) / (1.0 + 0.45 * qvs), -qc)
        t, qv, qc = t + 0.8 * cond, qv - cond, qc + cond
        adjusted = (t, qv, qc, qr)
        level = (lax.broadcasted_iota(jnp.int32, (count, LANES), 0) + base).astype(jnp.float32)
        height = level * (LOG2E / levels) - 1.0
        for substep in range(NSUB):
            qvs = jnp.exp2((0.3 * LOG2E) * t)
            log_rain = jnp.log2(qr)
            collected = 0.5 * jnp.maximum(qc - 0.5, 0.0) + 1.5 * qc * jnp.exp2(0.875 * log_rain)
            sink = jnp.minimum(collected, qc)
            evap = factor * jnp.maximum(qvs - qv, 0.0) * jnp.exp2(0.525 * log_rain)
            evap = jnp.minimum(evap, qr)
            t = t - 0.8 * evap
            qv = qv + evap
            qc = qc - sink
            mid = (qr + sink) - evap
            fall = jnp.minimum(jnp.exp2(0.1364 * jnp.log2(mid) + height), 0.9) * mid
            top = above[substep]
            if top is None:
                top = jnp.zeros((1, LANES), jnp.float32)
            inflow = jnp.concatenate([fall[1:], top], axis=0)
            above[substep] = fall[:1]
            qr = (mid - fall) + falloff * inflow
        rained = (t, qv, qc, qr)
        for f in range(4):
            rows = pl.ds(stride * base + 4 * k + f, count, stride=stride)
            if listed is None:
                tend_ref[rows, :] = rained[f] - before[f]
                dry_ref[rows, :] = adjusted[f] - before[f]
            else:
                after = jnp.where(listed[:count], rained[f], adjusted[f])
                tend_ref[rows, :] = after - before[f]


def inner_cells(
    edge_ref,
    sten_ref,
    rbf_ref,
    state_ref,
    tend_ref,
    dry_ref,
    wide_ref,
    part_ref,
    edge_table_ref,
    pos_ref,
    zon_ref,
    mer_ref,
    tmp_ref,
    table_ref,
):
    levels, edges = edge_ref.shape
    members, cells = sten_ref.shape
    blocks = cells // LANES
    halo = edge_table_ref.shape[1]
    window = table_ref.shape[0]
    fold = 2 * halo + ROWS
    tend_rows = tend_ref.reshape(tend_ref.shape[0] * 4 * blocks, LANES)
    dry_rows = dry_ref.reshape(dry_ref.shape[0] * 4 * blocks, LANES)
    merge_members(sten_ref, rbf_ref, pos_ref, zon_ref, mer_ref, tmp_ref, fold)

    def table(k):
        build_table(k, members, blocks, fold, window, pos_ref, zon_ref, mer_ref, table_ref)

    def inside(k, carry):
        table(k)
        start = pl.multiple_of(3 * LANES * k - halo, LANES)
        wind = jnp.dot(
            edge_ref[:, pl.ds(start, window)], table_ref[...], preferred_element_type=jnp.float32
        )
        keep_wind(k, levels, blocks, wind, wide_ref)
        rain_column(k, levels, blocks, None, wind, state_ref, tend_rows, dry_rows)
        return carry

    lax.fori_loop(1, blocks - 1, inside, 0)

    def border(side, carry):
        table(side * (blocks - 1))
        keep = pl.multiple_of(side * (window - halo), LANES)
        rest = pl.multiple_of((1 - side) * halo, LANES)
        start = pl.multiple_of(side * (edges - window + halo), LANES)
        edge_table_ref[side] = table_ref[pl.ds(keep, halo), :]
        part_ref[side] = jnp.dot(
            edge_ref[:, pl.ds(start, window - halo)],
            table_ref[pl.ds(rest, window - halo), :],
            preferred_element_type=jnp.float32,
        )
        return carry

    lax.fori_loop(0, 2, border, 0)


def is_early():
    dom, bal = lax.axis_index("dom"), lax.axis_index("bal")
    return jnp.logical_and(lax.rem(dom, RING) == 0, dom + bal > 0)


def first_kernel(*refs):
    sources, refs = refs[:6], refs[6:]
    left_ref, right_ref = refs[:2]
    held, results, refs = refs[2:7], refs[7:12], refs[12:]
    send_ref, work, sem = refs[0], refs[3:8], refs[8]
    edge_in, rest_in = sources[1], sources[2:]
    edge_ref = held[0]
    edges = edge_ref.shape[1]
    span = edges // PIECES
    first = pltpu.make_async_copy(sources[0], send_ref, sem.at[0])
    first.start()
    arrivals = []
    for piece in range(PIECES):
        part = pl.ds(piece * span, span)
        arrivals.append(
            pltpu.make_async_copy(edge_in.at[:, part], edge_ref.at[:, part], sem.at[1 + piece])
        )
        arrivals[-1].start()
    others = []
    for n, (source, target) in enumerate(zip(rest_in, held[1:])):
        part = pl.ds(0, source.shape[0])
        others.append(pltpu.make_async_copy(source, target.at[part], sem.at[1 + PIECES + n]))
        others[-1].start()
    first.wait()
    pick_sends(send_ref, edge_ref, arrivals, left_ref, right_ref, *refs[1:3])
    for copy in others:
        copy.wait()

    @pl.when(is_early())
    def _():
        inner_cells(*held[:4], *results, *work)


def second_kernel(*refs):
    held, count_ref, left_ref, refs = refs[:5], refs[5], refs[6], refs[12:]
    results, mask_ref, work = refs[:5], refs[5], refs[6:]
    tend_ref, dry_ref, wide_ref, part_ref, edge_table_ref = results
    levels = left_ref.shape[0]
    blocks = mask_ref.shape[0]

    @pl.when(jnp.logical_not(is_early()))
    def _():
        inner_cells(*held[:4], *results, *work)

    mask = listed_mask(held[4], count_ref[0])
    mask_ref[...] = mask
    group = 8
    fields = group // 2
    listed = [
        jnp.concatenate(
            [
                jnp.broadcast_to(mask[k : k + 1], (fields, LANES)),
                jnp.broadcast_to(mask[k + 1 : k + 2], (fields, LANES)),
            ],
            axis=0,
        )
        > 0.5
        for k in range(0, blocks, 2)
    ]

    def choose(level, carry):
        for n, here in enumerate(listed):
            rows = slice(group * n, group * (n + 1))
            tend_ref[level, rows] = jnp.where(here, tend_ref[level, rows], dry_ref[level, rows])
        return carry

    lax.fori_loop(0, levels, choose, 0, unroll=5)
    wind = part_ref[0] + jnp.dot(
        left_ref[...], edge_table_ref[0], preferred_element_type=jnp.float32
    )
    tend_rows = tend_ref.reshape(tend_ref.shape[0] * 4 * blocks, LANES)
    keep_wind(0, levels, blocks, wind, wide_ref)
    rain_column(0, levels, blocks, mask[:1], wind, held[3], tend_rows, None)


def outer_kernel(
    right_ref,
    part_ref,
    edge_table_ref,
    mask_ref,
    state_ref,
    tend_in,
    wide_in,
    tend_out,
    wind_out,
    tend_ref,
    wide_ref,
    wind_ref,
    sem,
):
    del tend_in, wide_in
    levels = right_ref.shape[0]
    blocks = mask_ref.shape[0]
    group = 8
    last = blocks - 1

    def send(first, count, n):
        part = pl.ds(first, count)
        copy = pltpu.make_async_copy(
            tend_ref.at[pl.ds(0, levels), part], tend_out.at[:, part], sem.at[n]
        )
        copy.start()
        return copy

    copies = [send(0, 4 * blocks - group, 0)]
    wind = part_ref[1] + jnp.dot(
        right_ref[...], edge_table_ref[1], preferred_element_type=jnp.float32
    )
    keep_wind(last, levels, blocks, wind, wide_ref)
    for level in range(levels):
        rows = slice(2 * blocks * level, 2 * blocks * (level + 1))
        wind_ref[rows, :] = wide_ref[rows, :].astype(jnp.bfloat16)
    copies.append(pltpu.make_async_copy(wind_ref, wind_out, sem.at[1]))
    copies[-1].start()
    tend_rows = tend_ref.reshape(tend_ref.shape[0] * 4 * blocks, LANES)
    rain_column(last, levels, blocks, mask_ref[last:blocks, :], wind, state_ref, tend_rows, None)
    copies.append(send(4 * blocks - group, group, 2))
    for copy in copies:
        copy.wait()


def local(edge_wind, send_edges, stencil, rbf_coeff, state, rain_cols, rain_count):
    levels, edges = edge_wind.shape
    halo = send_edges.shape[1]
    members, cells = stencil.shape
    blocks = cells // LANES
    slots = rain_cols.shape[0]
    padded = -(-levels // 8) * 8
    window = 3 * LANES + 2 * halo
    vmem = pl.BlockSpec(memory_space=pltpu.VMEM)
    anywhere = pl.BlockSpec(memory_space=pltpu.HBM)
    f32, bf16, i32 = jnp.float32, jnp.bfloat16, jnp.int32
    shape = jax.ShapeDtypeStruct
    state_rows = jnp.transpose(state.reshape(4, levels, blocks, LANES), (1, 2, 0, 3)).reshape(
        levels * blocks * 4, LANES
    )
    rbf_rows = jnp.transpose(rbf_coeff.reshape(2, members, blocks, LANES), (1, 2, 0, 3)).reshape(
        members * blocks * 2, LANES
    )
    held_shapes = [
        shape((levels, edges), bf16),
        shape((members, cells), i32),
        shape((members * blocks * 2, LANES), f32),
        shape((padded * blocks * 4, LANES), f32),
        shape((1, slots), i32),
    ]
    result_shapes = [
        shape((padded, blocks * 4, LANES), f32),
        shape((padded, blocks * 4, LANES), f32),
        shape((padded * blocks * 2, LANES), f32),
        shape((2, levels, 2 * LANES), f32),
        shape((2, halo, 2 * LANES), bf16),
    ]
    work = [
        pltpu.VMEM((members * blocks, LANES), i32),
        pltpu.VMEM((members * blocks, LANES), f32),
        pltpu.VMEM((members * blocks, LANES), f32),
        pltpu.VMEM((ROWS * blocks, LANES), i32),
        pltpu.VMEM((window, 2 * LANES), bf16),
    ]
    params = pltpu.CompilerParams(vmem_limit_bytes=VMEM_BYTES)
    first = pl.pallas_call(
        first_kernel,
        out_shape=[shape((levels, halo), bf16)] * 2 + held_shapes + result_shapes,
        in_specs=[anywhere] * 6,
        out_specs=[vmem] * 12,
        scratch_shapes=[
            pltpu.VMEM((2, halo), i32),
            pltpu.VMEM((edges // 256 * 64, 256), bf16),
            pltpu.VMEM((edges // 256 * 64, halo), f32),
        ]
        + work
        + [pltpu.SemaphoreType.DMA((1 + PIECES + 4,))],
        compiler_params=params,
        name="first_cells",
    )(
        *[
            pltpu.with_memory_space_constraint(array, pltpu.HBM)
            for array in (
                send_edges,
                edge_wind,
                stencil,
                rbf_rows,
                state_rows,
                rain_cols.reshape(1, slots),
            )
        ],
    )
    toward_left, toward_right = first[:2]
    held, results = first[2:7], first[7:]
    count = lax.axis_size("dom")
    from_left = lax.ppermute(toward_right, "dom", [(i, (i + 1) % count) for i in range(count)])
    from_right = lax.ppermute(toward_left, "dom", [((i + 1) % count, i) for i in range(count)])
    tend, _, wide, part, edge_table, mask = pl.pallas_call(
        second_kernel,
        out_shape=result_shapes + [shape((blocks, LANES), f32)],
        in_specs=[vmem] * 5 + [pl.BlockSpec(memory_space=pltpu.SMEM)] + [vmem] * 6,
        out_specs=[vmem] * 6,
        scratch_shapes=work,
        input_output_aliases={7 + n: n for n in range(5)},
        compiler_params=params,
        name="second_cells",
    )(*held, rain_count, from_left, *results)
    tend, wind, _, _ = pl.pallas_call(
        outer_kernel,
        out_shape=[
            shape((levels, blocks * 4, LANES), f32),
            shape((levels * blocks * 2, LANES), bf16),
            result_shapes[0],
            result_shapes[2],
        ],
        in_specs=[vmem] * 7,
        out_specs=[anywhere] * 2 + [vmem] * 2,
        scratch_shapes=[
            pltpu.VMEM((levels * blocks * 2, LANES), bf16),
            pltpu.SemaphoreType.DMA((3,)),
        ],
        input_output_aliases={5: 2, 6: 3},
        compiler_params=params,
        name="outer_cells",
    )(from_right, part, edge_table, mask, held[3], tend, wide)
    tendency = jnp.transpose(tend.reshape(levels, blocks, 4, LANES), (2, 0, 1, 3)).reshape(
        4, levels, cells
    )
    cell_wind = jnp.transpose(wind.reshape(levels, blocks, 2, LANES), (2, 0, 1, 3)).reshape(
        2, levels, cells
    )
    return (cell_wind, tendency)


def solution(mesh):
    placed = (
        P(None, ("dom", "bal")),
        P(None, ("dom", "bal")),
        P(None, ("dom", "bal")),
        P(None, None, ("dom", "bal")),
        P(None, None, ("dom", "bal")),
        P(("dom", "bal")),
        P(("dom", "bal")),
    )
    return jax.shard_map(
        local,
        mesh=mesh,
        in_specs=placed,
        out_specs=(P(None, None, ("dom", "bal")), P(None, None, ("dom", "bal"))),
        check_vma=False,
    )
```

time: 114 us -> 20.4 us (0.18)
  local copies, waits for them, and re-layouts: 50.7 us -> 0 us
  other arithmetic: 19.1 us -> 0 us
  loops' own time: 10.3 us -> 0 us
  starting transfers between devices: 20.8 us -> 11 us
  matrix products: 8.24 us -> 0 us
  Pallas kernels: 0 us -> 7.92 us
  waiting for transfers between devices: 1.9 us -> 0.01 us
    dynamic_update_slice x16 -> x0, local copies, waits for them, and re-layouts: 18.7 us -> none  [reconstruct(): blocks = lax.map(one_block, jnp.arange(block_total, dtype=jnp.int32))]
    another operation x1 -> x0, loops' own time: 10.3 us -> none  [reconstruct(): blocks = lax.map(one_block, jnp.arange(block_total, dtype=jnp.int32))]
    ppermute x4 -> x2, starting transfers between devices: 20.8 us -> 11 us  [the longest x1 9.07 us: local(): lax.ppermute(toward_left, 'dom', [((i + 1) % count, i) for i in range(cou...]
    dot_general x11 -> x0, matrix products: 8.24 us -> none  [the longest x8 3.51 us: one_block(): jnp.dot(edge_window, tables, precision=lax.Precision.HIGHEST, preferred_e...]
    pallas_call x0 -> x3, Pallas kernels: none -> 7.92 us  [the longest x1 6.15 us: local(): pl.pallas_call(first_kernel, out_shape=[shape((levels, halo), bf16)] * 2...]
    reduce_sum x8 -> x0, other arithmetic: 7.73 us -> none  [one_block(): zonal_table = jnp.sum(weights[0][:, None, :] * selector, axis=0)]
    slice x10 -> x0, local copies, waits for them, and re-layouts: 7.71 us -> none  [the longest x8 6.9 us: one_block(): meridional_table = jnp.sum(weights[1][:, None, :] * selector, axis=0)]
    sub x10 -> x0, other arithmetic: 7.05 us -> none  [the longest x8 5.68 us: one_block(): lax.dynamic_slice_in_dim(stencil, first_cell, block_cells, 1) - first_edge]
  transfers between devices with their start and end apart: 4 -> 2, of which waited for: 2 -> 0; matrix products, arithmetic and copies ran while one was open for 5% -> 0% of each run, Pallas kernels for 0% -> 3%
where the time goes in v1:
time: 20.4 us; the launch traced here: 20.2 us
  starting transfers between devices  11 us (54%)
  Pallas kernels  7.92 us (39%)
  between operations  1.33 us (7%)
    ppermute x1, starting transfers between devices, local(): lax.ppermute(toward_left, 'dom', [((i + 1) % count, i) for i in range(cou...  9.07 us
    pallas_call x1, Pallas kernels, local(): pl.pallas_call(first_kernel, out_shape=[shape((levels, halo), bf16)] * 2...  6.15 us
    ppermute x1, starting transfers between devices, local(): lax.ppermute(toward_right, 'dom', [(i, (i + 1) % count) for i in range(co...  1.92 us
    pallas_call x1, Pallas kernels, local(): pl.pallas_call(outer_kernel, out_shape=[shape((levels, blocks * 4, LANES)...  1.1 us
    pallas_call x1, Pallas kernels, local(): pl.pallas_call(second_kernel, out_shape=result_shapes + [shape((blocks, L...  0.67 us
  transfers between devices with their start and end apart: 2, of which 0 were waited for; matrix products, arithmetic and copies ran while one was open for 0% of the time, Pallas kernels for 3%

profile of v1, /device:TPU:1, one launch (start us, length us, event | category | flops | bytes accessed | tf_op | source)
XLA Modules:
  0.0 20.2 jit_solution(11325973787786001788)
XLA Ops:
  0.6 6.1 %first_cells.1 = (bf16[55,256]{1,0:T(8,128)(2,1)S(1)}, bf16[55,256]{1,0:T(8,128)(2,1)S(1)}, bf16[55,3072]{1,0:T(8,128)(2,1)S(1)}, s32[10,1024]{1,0:T(8,128)S(1)}...) custom-call(s32[2,256]{1,0:T(2,128)} %refs_0_.1, ...), custom_call_target="tpu_custom_call" | custom-call | tf_op jit(solution)/shard_map/first_cells/pallas_call | solution.py:409
  6.8 1.9 %collective-permute-start.1 = (bf16[55,256]{1,0:T(8,128)(2,1)S(1)}, bf16[55,256]{1,0:T(8,128)(2,1)S(1)}, u32[]{:S(2)}, u32[]{:S(2)}) collective-permute-start(bf16[55,256]{1,0:T(8,128)(2,1)S(1)} %get-tuple-element.27), channel_id=1, source_target_pairs={{0,16},{16,32},{32,48},{48,64},{64,80},{80,96},{96,112},{112,128},... | collective-permute-start | bytes 84488 | tf_op jit(solution)/shard_map/ppermute | solution.py:439
  8.7 9.1 %collective-permute-start = (bf16[55,256]{1,0:T(8,128)(2,1)S(1)}, bf16[55,256]{1,0:T(8,128)(2,1)S(1)}, u32[]{:S(2)}, u32[]{:S(2)}) collective-permute-start(bf16[55,256]{1,0:T(8,128)(2,1)S(1)} %get-tuple-element.21), channel_id=1, source_target_pairs={{16,0},{32,16},{48,32},{64,48},{80,64},{96,80},{112,96},{128,112},... | collective-permute-start | bytes 84488 | tf_op jit(solution)/shard_map/ppermute | solution.py:440
  18.4 0.0 collective-permute-done.1.refs_6_
  18.4 0.7 %second_cells.1 = (f32[56,32,128]{2,1,0:T(8,128)S(1)}, f32[56,32,128]{2,1,0:T(8,128)S(1)}, f32[896,128]{1,0:T(8,128)S(1)}, f32[2,55,256]{2,1,0:T(8,128)S(1)}, bf...) custom-call(bf16[55,3072]{1,0:T(8,128)(2,1)S(1)} %get-tuple-element., ...), custom_call_target="tpu_custom_call", output_to_operand_aliasing={{0}: (7, {}), {1}: (8, {}), {2}: (9, {}), {3}: (10, {}), {4... | custom-call | tf_op jit(solution)/shard_map/second_cells/pallas_call | solution.py:441
  19.1 0.0 collective-permute-done.right_ref
  19.1 1.1 %outer_cells.1 = (f32[55,32,128]{2,1,0:T(8,128)}, bf16[880,128]{1,0:T(8,128)(2,1)}, f32[56,32,128]{2,1,0:T(8,128)S(1)}, f32[896,128]{1,0:T(8,128)S(1)}) custom-call(bf16[55,256]{1,0:T(8,128)(2,1)S(1)} %collective-permute-done.right_ref, f32[2,55,256]{2,1,0:T(8,128)S(1)} %get-tuple-element.33.part_ref, ...), custom_call_target="tpu_custom_call", output_to_operand_aliasing={{2}: (5, {}), {3}: (6, {})} | custom-call | tf_op jit(solution)/shard_map/outer_cells/pallas_call | solution.py:451
Async XLA Ops:
  6.8 11.7 %collective-permute-start.1 = (bf16[55,256]{1,0:T(8,128)(2,1)S(1)}, bf16[55,256]{1,0:T(8,128)(2,1)S(1)}, u32[]{:S(2)}, u32[]{:S(2)}) collective-permute-start(bf16[55,256]{1,0:T(8,128)(2,1)S(1)} %get-tuple-element.27), channel_id=1, source_target_pairs={{0,16},{16,32},{32,48},{48,64},{64,80},{80,96},{96,112},{112,128},... | collective-permute-start | bytes 84488 | tf_op jit(solution)/shard_map/ppermute | solution.py:439
  8.7 10.4 %collective-permute-start = (bf16[55,256]{1,0:T(8,128)(2,1)S(1)}, bf16[55,256]{1,0:T(8,128)(2,1)S(1)}, u32[]{:S(2)}, u32[]{:S(2)}) collective-permute-start(bf16[55,256]{1,0:T(8,128)(2,1)S(1)} %get-tuple-element.21), channel_id=1, source_target_pairs={{16,0},{32,16},{48,32},{64,48},{80,64},{96,80},{112,96},{128,112},... | collective-permute-start | bytes 84488 | tf_op jit(solution)/shard_map/ppermute | solution.py:440

commit v2 on v1

--- a/solution.py
+++ b/solution.py
@@ -11,7 +11,7 @@
 LOG2E = math.log2(math.e)
 LANES = 128
 ROWS = 16
-PIECES = 4
+PIECES = 1
 VMEM_BYTES = 40 * 1024 * 1024
 RING = 8
 
@@ -39,19 +39,17 @@
             arrivals[first // span].wait()
         base = first // chunk * step
         stack_ref[base : base + levels, :] = edge_ref[:, first : first + chunk]
-    for side, out_ref in ((0, left_ref), (1, right_ref)):
-        columns = slice(side * width, (side + 1) * width)
-        found_ref[...] = jnp.dot(
-            stack_ref[...], picker[:, columns], preferred_element_type=jnp.float32
-        )
-        here = [high[:, columns] == n for n in range(edges // chunk)]
-        total = []
-        for base in range(0, levels, 8):
-            some = found_ref[base : base + 8, :]
-            for n in range(1, edges // chunk):
-                some = jnp.where(here[n], found_ref[n * step + base : n * step + base + 8, :], some)
-            total.append(some)
-        out_ref[...] = jnp.concatenate(total, axis=0)[:levels].astype(jnp.bfloat16)
+    found_ref[...] = jnp.dot(stack_ref[...], picker, preferred_element_type=jnp.float32)
+    here = [high == n for n in range(edges // chunk)]
+    total = []
+    for base in range(0, levels, 8):
+        some = found_ref[base : base + 8, :]
+        for n in range(1, edges // chunk):
+            some = jnp.where(here[n], found_ref[n * step + base : n * step + base + 8, :], some)
+        total.append(some)
+    total = jnp.concatenate(total, axis=0)[:levels].astype(jnp.bfloat16)
+    left_ref[...] = total[:, :width]
+    right_ref[...] = total[:, width:]
 
 
 def listed_mask(cols_ref, count):
@@ -254,8 +252,6 @@
     edge_ref = held[0]
     edges = edge_ref.shape[1]
     span = edges // PIECES
-    first = pltpu.make_async_copy(sources[0], send_ref, sem.at[0])
-    first.start()
     arrivals = []
     for piece in range(PIECES):
         part = pl.ds(piece * span, span)
@@ -263,6 +259,8 @@
             pltpu.make_async_copy(edge_in.at[:, part], edge_ref.at[:, part], sem.at[1 + piece])
         )
         arrivals[-1].start()
+    first = pltpu.make_async_copy(sources[0], send_ref, sem.at[0])
+    first.start()
     others = []
     for n, (source, target) in enumerate(zip(rest_in, held[1:])):
         part = pl.ds(0, source.shape[0])
@@ -414,7 +412,7 @@
         scratch_shapes=[
             pltpu.VMEM((2, halo), i32),
             pltpu.VMEM((edges // 256 * 64, 256), bf16),
-            pltpu.VMEM((edges // 256 * 64, halo), f32),
+            pltpu.VMEM((edges // 256 * 64, 2 * halo), f32),
         ]
         + work
         + [pltpu.SemaphoreType.DMA((1 + PIECES + 4,))],

time: 20.4 us -> 20.3 us (level)
  no operation moved by 1% of the time
where the time goes in v2:
time: 20.3 us; the launch traced here: 20.1 us
  starting transfers between devices  11 us (54%)
  Pallas kernels  7.83 us (39%)
  between operations  1.33 us (7%)
    ppermute x1, starting transfers between devices, local(): lax.ppermute(toward_left, 'dom', [((i + 1) % count, i) for i in range(cou...  9.07 us
    pallas_call x1, Pallas kernels, local(): pl.pallas_call(first_kernel, out_shape=[shape((levels, halo), bf16)] * 2...  6.06 us
    ppermute x1, starting transfers between devices, local(): lax.ppermute(toward_right, 'dom', [(i, (i + 1) % count) for i in range(co...  1.92 us
    pallas_call x1, Pallas kernels, local(): pl.pallas_call(outer_kernel, out_shape=[shape((levels, blocks * 4, LANES)...  1.1 us
    pallas_call x1, Pallas kernels, local(): pl.pallas_call(second_kernel, out_shape=result_shapes + [shape((blocks, L...  0.67 us
  transfers between devices with their start and end apart: 2, of which 0 were waited for; matrix products, arithmetic and copies ran while one was open for 0% of the time, Pallas kernels for 3%

profile of v2, /device:TPU:1, one launch (start us, length us, event | category | flops | bytes accessed | tf_op | source)
XLA Modules:
  0.0 20.1 jit_solution(7114834805761546967)
XLA Ops:
  0.6 6.1 %first_cells.1 = (bf16[55,256]{1,0:T(8,128)(2,1)S(1)}, bf16[55,256]{1,0:T(8,128)(2,1)S(1)}, bf16[55,3072]{1,0:T(8,128)(2,1)S(1)}, s32[10,1024]{1,0:T(8,128)S(1)}...) custom-call(s32[2,256]{1,0:T(2,128)} %refs_0_.1, ...), custom_call_target="tpu_custom_call" | custom-call | tf_op jit(solution)/shard_map/first_cells/pallas_call | solution.py:407
  6.7 1.9 %collective-permute-start.1 = (bf16[55,256]{1,0:T(8,128)(2,1)S(1)}, bf16[55,256]{1,0:T(8,128)(2,1)S(1)}, u32[]{:S(2)}, u32[]{:S(2)}) collective-permute-start(bf16[55,256]{1,0:T(8,128)(2,1)S(1)} %get-tuple-element.27), channel_id=1, source_target_pairs={{0,16},{16,32},{32,48},{48,64},{64,80},{80,96},{96,112},{112,128},... | collective-permute-start | bytes 84488 | tf_op jit(solution)/shard_map/ppermute | solution.py:437
  8.6 9.1 %collective-permute-start = (bf16[55,256]{1,0:T(8,128)(2,1)S(1)}, bf16[55,256]{1,0:T(8,128)(2,1)S(1)}, u32[]{:S(2)}, u32[]{:S(2)}) collective-permute-start(bf16[55,256]{1,0:T(8,128)(2,1)S(1)} %get-tuple-element.21), channel_id=1, source_target_pairs={{16,0},{32,16},{48,32},{64,48},{80,64},{96,80},{112,96},{128,112},... | collective-permute-start | bytes 84488 | tf_op jit(solution)/shard_map/ppermute | solution.py:438
  18.3 0.0 collective-permute-done.1.refs_6_
  18.4 0.7 %second_cells.1 = (f32[56,32,128]{2,1,0:T(8,128)S(1)}, f32[56,32,128]{2,1,0:T(8,128)S(1)}, f32[896,128]{1,0:T(8,128)S(1)}, f32[2,55,256]{2,1,0:T(8,128)S(1)}, bf...) custom-call(bf16[55,3072]{1,0:T(8,128)(2,1)S(1)} %get-tuple-element., ...), custom_call_target="tpu_custom_call", output_to_operand_aliasing={{0}: (7, {}), {1}: (8, {}), {2}: (9, {}), {3}: (10, {}), {4... | custom-call | tf_op jit(solution)/shard_map/second_cells/pallas_call | solution.py:439
  19.0 0.0 collective-permute-done.right_ref
  19.0 1.1 %outer_cells.1 = (f32[55,32,128]{2,1,0:T(8,128)}, bf16[880,128]{1,0:T(8,128)(2,1)}, f32[56,32,128]{2,1,0:T(8,128)S(1)}, f32[896,128]{1,0:T(8,128)S(1)}) custom-call(bf16[55,256]{1,0:T(8,128)(2,1)S(1)} %collective-permute-done.right_ref, f32[2,55,256]{2,1,0:T(8,128)S(1)} %get-tuple-element.33.part_ref, ...), custom_call_target="tpu_custom_call", output_to_operand_aliasing={{2}: (5, {}), {3}: (6, {})} | custom-call | tf_op jit(solution)/shard_map/outer_cells/pallas_call | solution.py:449
Async XLA Ops:
  6.7 11.7 %collective-permute-start.1 = (bf16[55,256]{1,0:T(8,128)(2,1)S(1)}, bf16[55,256]{1,0:T(8,128)(2,1)S(1)}, u32[]{:S(2)}, u32[]{:S(2)}) collective-permute-start(bf16[55,256]{1,0:T(8,128)(2,1)S(1)} %get-tuple-element.27), channel_id=1, source_target_pairs={{0,16},{16,32},{32,48},{48,64},{64,80},{80,96},{96,112},{112,128},... | collective-permute-start | bytes 84488 | tf_op jit(solution)/shard_map/ppermute | solution.py:437
  8.6 10.4 %collective-permute-start = (bf16[55,256]{1,0:T(8,128)(2,1)S(1)}, bf16[55,256]{1,0:T(8,128)(2,1)S(1)}, u32[]{:S(2)}, u32[]{:S(2)}) collective-permute-start(bf16[55,256]{1,0:T(8,128)(2,1)S(1)} %get-tuple-element.21), channel_id=1, source_target_pairs={{16,0},{32,16},{48,32},{64,48},{80,64},{96,80},{112,96},{128,112},... | collective-permute-start | bytes 84488 | tf_op jit(solution)/shard_map/ppermute | solution.py:438

commit v3 on v2

--- a/solution.py
+++ b/solution.py
@@ -243,6 +243,17 @@
     return jnp.logical_and(lax.rem(dom, RING) == 0, dom + bal > 0)
 
 
+def is_latest():
+    return lax.rem(lax.axis_index("dom"), RING) == RING - 1
+
+
+def fetches(sources, targets, sem, base):
+    return [
+        pltpu.make_async_copy(source, target.at[pl.ds(0, source.shape[0])], sem.at[base + n])
+        for n, (source, target) in enumerate(zip(sources, targets))
+    ]
+
+
 def first_kernel(*refs):
     sources, refs = refs[:6], refs[6:]
     left_ref, right_ref = refs[:2]
@@ -261,15 +272,20 @@
         arrivals[-1].start()
     first = pltpu.make_async_copy(sources[0], send_ref, sem.at[0])
     first.start()
-    others = []
-    for n, (source, target) in enumerate(zip(rest_in, held[1:])):
-        part = pl.ds(0, source.shape[0])
-        others.append(pltpu.make_async_copy(source, target.at[part], sem.at[1 + PIECES + n]))
-        others[-1].start()
+    others = fetches(rest_in, held[1:], sem, 1 + PIECES)
+
+    @pl.when(jnp.logical_not(is_latest()))
+    def _():
+        for copy in others:
+            copy.start()
+
     first.wait()
     pick_sends(send_ref, edge_ref, arrivals, left_ref, right_ref, *refs[1:3])
-    for copy in others:
-        copy.wait()
+
+    @pl.when(jnp.logical_not(is_latest()))
+    def _():
+        for copy in others:
+            copy.wait()
 
     @pl.when(is_early())
     def _():
@@ -277,11 +293,20 @@
 
 
 def second_kernel(*refs):
-    held, count_ref, left_ref, refs = refs[:5], refs[5], refs[6], refs[12:]
-    results, mask_ref, work = refs[:5], refs[5], refs[6:]
+    edge_ref, count_ref, left_ref, sources, refs = refs[0], refs[1], refs[2], refs[3:7], refs[16:]
+    results, mask_ref, held, refs = refs[:5], refs[5], (edge_ref, *refs[6:10]), refs[10:]
+    work, sem = refs[:5], refs[5]
     tend_ref, dry_ref, wide_ref, part_ref, edge_table_ref = results
     levels = left_ref.shape[0]
     blocks = mask_ref.shape[0]
+    others = fetches(sources, held[1:], sem, 0)
+
+    @pl.when(is_latest())
+    def _():
+        for copy in others:
+            copy.start()
+        for copy in others:
+            copy.wait()
 
     @pl.when(jnp.logical_not(is_early()))
     def _():
@@ -404,6 +429,17 @@
         pltpu.VMEM((window, 2 * LANES), bf16),
     ]
     params = pltpu.CompilerParams(vmem_limit_bytes=VMEM_BYTES)
+    sources = [
+        pltpu.with_memory_space_constraint(array, pltpu.HBM)
+        for array in (
+            send_edges,
+            edge_wind,
+            stencil,
+            rbf_rows,
+            state_rows,
+            rain_cols.reshape(1, slots),
+        )
+    ]
     first = pl.pallas_call(
         first_kernel,
         out_shape=[shape((levels, halo), bf16)] * 2 + held_shapes + result_shapes,
@@ -418,34 +454,22 @@
         + [pltpu.SemaphoreType.DMA((1 + PIECES + 4,))],
         compiler_params=params,
         name="first_cells",
-    )(
-        *[
-            pltpu.with_memory_space_constraint(array, pltpu.HBM)
-            for array in (
-                send_edges,
-                edge_wind,
-                stencil,
-                rbf_rows,
-                state_rows,
-                rain_cols.reshape(1, slots),
-            )
-        ],
-    )
+    )(*sources)
     toward_left, toward_right = first[:2]
     held, results = first[2:7], first[7:]
     count = lax.axis_size("dom")
     from_left = lax.ppermute(toward_right, "dom", [(i, (i + 1) % count) for i in range(count)])
     from_right = lax.ppermute(toward_left, "dom", [((i + 1) % count, i) for i in range(count)])
-    tend, _, wide, part, edge_table, mask = pl.pallas_call(
+    tend, _, wide, part, edge_table, mask, _, _, state_held, _ = pl.pallas_call(
         second_kernel,
-        out_shape=result_shapes + [shape((blocks, LANES), f32)],
-        in_specs=[vmem] * 5 + [pl.BlockSpec(memory_space=pltpu.SMEM)] + [vmem] * 6,
-        out_specs=[vmem] * 6,
-        scratch_shapes=work,
-        input_output_aliases={7 + n: n for n in range(5)},
+        out_shape=result_shapes + [shape((blocks, LANES), f32)] + held_shapes[1:],
+        in_specs=[vmem, pl.BlockSpec(memory_space=pltpu.SMEM), vmem] + [anywhere] * 4 + [vmem] * 9,
+        out_specs=[vmem] * 10,
+        scratch_shapes=work + [pltpu.SemaphoreType.DMA((4,))],
+        input_output_aliases={7 + n: 6 + n for n in range(4)} | {11 + n: n for n in range(5)},
         compiler_params=params,
         name="second_cells",
-    )(*held, rain_count, from_left, *results)
+    )(held[0], rain_count, from_left, *sources[2:], *held[1:], *results)
     tend, wind, _, _ = pl.pallas_call(
         outer_kernel,
         out_shape=[
@@ -463,7 +487,7 @@
         input_output_aliases={5: 2, 6: 3},
         compiler_params=params,
         name="outer_cells",
-    )(from_right, part, edge_table, mask, held[3], tend, wide)
+    )(from_right, part, edge_table, mask, state_held, tend, wide)
     tendency = jnp.transpose(tend.reshape(levels, blocks, 4, LANES), (2, 0, 1, 3)).reshape(
         4, levels, cells
     )

time: 20.3 us -> 20.4 us (level)
  transfers between devices with their start and end apart: 2 -> 2, of which waited for: 0 -> 0; matrix products, arithmetic and copies ran while one was open for 0% -> 0% of each run, Pallas kernels for 3% -> 4%
where the time goes in v3:
time: 20.4 us; the launch traced here: 20.2 us
  starting transfers between devices  11 us (54%)
  Pallas kernels  7.89 us (39%)
  between operations  1.32 us (6%)
    ppermute x1, starting transfers between devices, local(): lax.ppermute(toward_left, 'dom', [((i + 1) % count, i) for i in range(cou...  9.04 us
    pallas_call x1, Pallas kernels, local(): pl.pallas_call(first_kernel, out_shape=[shape((levels, halo), bf16)] * 2...  6.06 us
    ppermute x1, starting transfers between devices, local(): lax.ppermute(toward_right, 'dom', [(i, (i + 1) % count) for i in range(co...  1.92 us
    pallas_call x1, Pallas kernels, local(): pl.pallas_call(outer_kernel, out_shape=[shape((levels, blocks * 4, LANES)...  1.1 us
    pallas_call x1, Pallas kernels, local(): pl.pallas_call(second_kernel, out_shape=result_shapes + [shape((blocks, L...  0.73 us
  transfers between devices with their start and end apart: 2, of which 0 were waited for; matrix products, arithmetic and copies ran while one was open for 0% of the time, Pallas kernels for 4%

profile of v3, /device:TPU:1, one launch (start us, length us, event | category | flops | bytes accessed | tf_op | source)
XLA Modules:
  0.0 20.2 jit_solution(7700545087377428686)
XLA Ops:
  0.6 6.1 %first_cells.1 = (bf16[55,256]{1,0:T(8,128)(2,1)S(1)}, bf16[55,256]{1,0:T(8,128)(2,1)S(1)}, bf16[55,3072]{1,0:T(8,128)(2,1)S(1)}, s32[10,1024]{1,0:T(8,128)S(1)}...) custom-call(s32[2,256]{1,0:T(2,128)} %refs_0_.1, ...), custom_call_target="tpu_custom_call" | custom-call | tf_op jit(solution)/shard_map/first_cells/pallas_call | solution.py:443
  6.7 1.9 %collective-permute-start.1 = (bf16[55,256]{1,0:T(8,128)(2,1)S(1)}, bf16[55,256]{1,0:T(8,128)(2,1)S(1)}, u32[]{:S(2)}, u32[]{:S(2)}) collective-permute-start(bf16[55,256]{1,0:T(8,128)(2,1)S(1)} %get-tuple-element.24), channel_id=1, source_target_pairs={{0,16},{16,32},{32,48},{48,64},{64,80},{80,96},{96,112},{112,128},... | collective-permute-start | bytes 84488 | tf_op jit(solution)/shard_map/ppermute | solution.py:461
  8.6 9.0 %collective-permute-start = (bf16[55,256]{1,0:T(8,128)(2,1)S(1)}, bf16[55,256]{1,0:T(8,128)(2,1)S(1)}, u32[]{:S(2)}, u32[]{:S(2)}) collective-permute-start(bf16[55,256]{1,0:T(8,128)(2,1)S(1)} %get-tuple-element.22), channel_id=1, source_target_pairs={{16,0},{32,16},{48,32},{64,48},{80,64},{96,80},{112,96},{128,112},... | collective-permute-start | bytes 84488 | tf_op jit(solution)/shard_map/ppermute | solution.py:462
  18.3 0.0 collective-permute-done.1.refs_2_
  18.3 0.7 %second_cells.1 = (f32[56,32,128]{2,1,0:T(8,128)S(1)}, f32[56,32,128]{2,1,0:T(8,128)S(1)}, f32[896,128]{1,0:T(8,128)S(1)}, f32[2,55,256]{2,1,0:T(8,128)S(1)}, bf...) custom-call(bf16[55,3072]{1,0:T(8,128)(2,1)S(1)} %get-tuple-element., ...), custom_call_target="tpu_custom_call", output_to_operand_aliasing={{6}: (7, {}), {7}: (8, {}), {8}: (9, {}), {9}: (10, {}), {0... | custom-call | tf_op jit(solution)/shard_map/second_cells/pallas_call | solution.py:463
  19.1 0.0 collective-permute-done.right_ref
  19.1 1.1 %outer_cells.1 = (f32[55,32,128]{2,1,0:T(8,128)}, bf16[880,128]{1,0:T(8,128)(2,1)}, f32[56,32,128]{2,1,0:T(8,128)S(1)}, f32[896,128]{1,0:T(8,128)S(1)}) custom-call(bf16[55,256]{1,0:T(8,128)(2,1)S(1)} %collective-permute-done.right_ref, f32[2,55,256]{2,1,0:T(8,128)S(1)} %get-tuple-element.34.part_ref, ...), custom_call_target="tpu_custom_call", output_to_operand_aliasing={{2}: (5, {}), {3}: (6, {})} | custom-call | tf_op jit(solution)/shard_map/outer_cells/pallas_call | solution.py:473
Async XLA Ops:
  6.7 11.6 %collective-permute-start.1 = (bf16[55,256]{1,0:T(8,128)(2,1)S(1)}, bf16[55,256]{1,0:T(8,128)(2,1)S(1)}, u32[]{:S(2)}, u32[]{:S(2)}) collective-permute-start(bf16[55,256]{1,0:T(8,128)(2,1)S(1)} %get-tuple-element.24), channel_id=1, source_target_pairs={{0,16},{16,32},{32,48},{48,64},{64,80},{80,96},{96,112},{112,128},... | collective-permute-start | bytes 84488 | tf_op jit(solution)/shard_map/ppermute | solution.py:461
  8.6 10.4 %collective-permute-start = (bf16[55,256]{1,0:T(8,128)(2,1)S(1)}, bf16[55,256]{1,0:T(8,128)(2,1)S(1)}, u32[]{:S(2)}, u32[]{:S(2)}) collective-permute-start(bf16[55,256]{1,0:T(8,128)(2,1)S(1)} %get-tuple-element.22), channel_id=1, source_target_pairs={{16,0},{32,16},{48,32},{64,48},{80,64},{96,80},{112,96},{128,112},... | collective-permute-start | bytes 84488 | tf_op jit(solution)/shard_map/ppermute | solution.py:462
